TPU v7x, 32 devices: a whole 2x2x4 slice. The times are simulated.
32 devices in a mesh: dp: 4 (over z), fsdp: 2 (over x), tensor: 4 (over y, core).
Axes of the slice: x: 2, y: 2, z: 4, core: 2. Of those that a mesh axis runs over, the one named last changes fastest.
Arguments:
- candidates: bfloat16 [4, 16, 64, 4096], P('dp', 'fsdp', None, 'tensor'), may hold values from -40 to 40
- cand_lengths: int32 [4, 16], P('dp', 'fsdp'), may hold values from 1 to 64, 768 in all within a row
- pairing: int32 [4, 8, 2], P('dp'), may hold values from 0 to 15, as said below
- attn_gain: float32 [4096], replicated, may hold values from 0.1 to 1.9
- w_query: bfloat16 [4096, 4096], P('fsdp', 'tensor'), may hold values from -2 to 2
- w_key: bfloat16 [4096, 512], P('fsdp', 'tensor'), may hold values from -1 to 1
- w_value: bfloat16 [4096, 512], P('fsdp', 'tensor'), may hold values from -0.09375 to 0.09375
- w_out: bfloat16 [4096, 4096], P('tensor', 'fsdp'), may hold values from -0.09375 to 0.09375
- ffn_gain: float32 [4096], replicated, may hold values from 0.1 to 1.9
Outputs:
- resid: bfloat16 [4, 8, 128, 4096], P('dp', 'fsdp', None, 'tensor')
- normed: bfloat16 [4, 8, 128, 4096], P('dp', 'fsdp')
Inputs may be any that keep to these rules, and one draw needn't show every extreme that they name: pairing[p] names each of the 16 candidates of prompt p exactly once. Candidates come in blocks of 8 consecutive indices and pair rows in blocks of 4; each block of candidates sends exactly 4 of its candidates to each of 2 blocks of pair rows.
All inputs are finite; a program needn't handle non-finite values. No bound on the sum of `cand_lengths` on one device may be relied on, other than what follows from the above.
Results may differ from a plain program's by a relative error of at most 0.018.
Values may be sent and summed in bfloat16 or wider, within the bound.
A program may use at most 192 MiB of HBM per device.

v0:
```python
import jax
import jax.numpy as jnp
from jax import lax
from jax.sharding import PartitionSpec as P

HEAD = 128


epsilon = 1e-05
rope_base = 500000.0


def rms_scale(values, gain):
    mean_square = jnp.mean(values * values, axis=-1, keepdims=True)
    return values * lax.rsqrt(mean_square + epsilon) * gain


def positions_of(lengths, sample):
    slot_steps = jnp.arange(2 * sample, dtype=jnp.int32)
    return jnp.where(slot_steps < sample, slot_steps, lengths[..., :1] + slot_steps - sample)


def key_mask(lengths, sample):
    slot_steps = jnp.arange(2 * sample, dtype=jnp.int32)
    local_step = jnp.where(slot_steps < sample, slot_steps, slot_steps - sample)
    limit = jnp.where(slot_steps < sample, lengths[..., :1], lengths[..., 1:])
    valid = local_step < limit
    causal = slot_steps[None, :] <= slot_steps[:, None]
    return causal[None] & valid[:, None, :]


def rotate(values, positions, head_size):
    half = head_size // 2
    inv_freq = rope_base ** (-jnp.arange(half, dtype=jnp.float32) * 2.0 / head_size)
    angles = positions.astype(jnp.float32)[..., None] * inv_freq
    cosine = jnp.cos(angles)[..., None, :]
    sine_table = jnp.sin(angles)[..., None, :]
    lower = values[..., :half]
    upper = values[..., half:]
    return jnp.concatenate(
        [lower * cosine - upper * sine_table, upper * cosine + lower * sine_table], axis=-1
    )


def attend(query, key_rows, value_rows, allowed):
    pair_rows, row_count, kv_count, group_size, head_size = query.shape
    scores = jnp.einsum(
        "bqkgd,bskd->bkgqs", query, key_rows, preferred_element_type=jnp.float32
    ) * head_size ** (-0.5)
    scores = jnp.where(allowed[:, None, None], scores, -1e30)
    row_peak = jnp.max(scores, axis=-1, keepdims=True)
    weights = jnp.exp(scores - row_peak)
    prob_rows = (weights / jnp.sum(weights, axis=-1, keepdims=True)).astype(jnp.bfloat16)
    mixed_rows = jnp.einsum(
        "bkgqs,bskd->bqkgd", prob_rows, value_rows, preferred_element_type=jnp.float32
    )
    return mixed_rows.astype(jnp.bfloat16).reshape(
        pair_rows * row_count, kv_count * group_size * head_size
    )


def on_device(
    candidates, cand_lengths, pairing, attn_gain, w_query, w_key, w_value, w_out, ffn_gain
):
    fsdp_count = lax.axis_size("fsdp")
    my_index = lax.axis_index("fsdp")
    cand_dev = candidates.shape[1]
    sample = candidates.shape[2]
    share_width = candidates.shape[3]
    pair_dev = cand_dev // 2
    most_slots = max(1, cand_dev // fsdp_count)
    flat_slots = pairing[0].reshape(-1)
    slot_count = flat_slots.shape[0]
    every_slot = jnp.arange(slot_count, dtype=jnp.int32)
    matches = flat_slots[:, None] == every_slot[None, :]
    target_slot = jnp.sum(jnp.where(matches, every_slot[:, None], 0), axis=0)
    target_dev = target_slot // cand_dev
    source_dev = every_slot // cand_dev
    earlier = (
        (source_dev[:, None] == source_dev[None, :])
        & (target_dev[:, None] == target_dev[None, :])
        & (every_slot[None, :] < every_slot[:, None])
    )
    send_rank = jnp.sum(earlier.astype(jnp.int32), axis=1)
    place = target_dev * most_slots + send_rank
    arrive = source_dev * most_slots + send_rank
    own_cands = my_index * cand_dev + jnp.arange(cand_dev, dtype=jnp.int32)
    own_pick = own_cands[:, None] == every_slot[None, :]
    own_place = jnp.sum(jnp.where(own_pick, place[None, :], 0), axis=1)
    buffer_slots = jnp.arange(fsdp_count * most_slots, dtype=jnp.int32)
    sender = buffer_slots[:, None] == own_place[None, :]
    outgoing = jnp.einsum(
        "bc,csf->bsf",
        sender.astype(jnp.bfloat16),
        candidates[0],
        preferred_element_type=jnp.float32,
    ).astype(jnp.bfloat16)
    out_lengths = jnp.sum(jnp.where(sender, cand_lengths[0][None, :], 0), axis=1)
    incoming, in_lengths = (
        lax.all_to_all(
            outgoing.reshape(fsdp_count, most_slots, sample, share_width),
            "fsdp",
            split_axis=0,
            concat_axis=0,
            tiled=True,
        ),
        lax.all_to_all(
            out_lengths.reshape(fsdp_count, most_slots),
            "fsdp",
            split_axis=0,
            concat_axis=0,
            tiled=True,
        ),
    )
    slot_pick = own_cands[:, None] == every_slot[None, :]
    wanted = jnp.sum(jnp.where(slot_pick, flat_slots[None, :], 0), axis=1)
    wanted_pick = wanted[:, None] == every_slot[None, :]
    wanted_from = jnp.sum(jnp.where(wanted_pick, arrive[None, :], 0), axis=1)
    receiver = wanted_from[:, None] == buffer_slots[None, :]
    local_rows = jnp.einsum(
        "cb,bsf->csf",
        receiver.astype(jnp.bfloat16),
        incoming.reshape(-1, sample, share_width),
        preferred_element_type=jnp.float32,
    ).astype(jnp.bfloat16)
    row_lengths = (
        jnp.sum(jnp.where(receiver, in_lengths.reshape(-1)[None, :], 0), axis=1)
        .astype(jnp.int32)
        .reshape(pair_dev, 2)
    )
    full_rows = lax.all_gather(local_rows, "tensor", axis=2, tiled=True)
    width = full_rows.shape[2]
    tok_count = cand_dev * sample
    inputs = full_rows.reshape(tok_count, width).astype(jnp.float32)
    normal_rows = rms_scale(inputs, attn_gain).astype(jnp.bfloat16)
    query_cols = w_query.shape[1]
    key_cols = w_key.shape[1]
    query = jnp.dot(
        normal_rows,
        lax.all_gather(w_query, "fsdp", axis=0, tiled=True),
        preferred_element_type=jnp.float32,
    )
    key_rows = jnp.dot(
        normal_rows,
        lax.all_gather(w_key, "fsdp", axis=0, tiled=True),
        preferred_element_type=jnp.float32,
    )
    value_rows = jnp.dot(
        normal_rows,
        lax.all_gather(w_value, "fsdp", axis=0, tiled=True),
        preferred_element_type=jnp.float32,
    )
    heads_here = query_cols // HEAD
    kv_here = key_cols // HEAD
    positions = positions_of(row_lengths, sample)
    query = rotate(query.reshape(pair_dev, 2 * sample, heads_here, HEAD), positions, HEAD).astype(
        jnp.bfloat16
    )
    key_rows = rotate(
        key_rows.reshape(pair_dev, 2 * sample, kv_here, HEAD), positions, HEAD
    ).astype(jnp.bfloat16)
    value_rows = value_rows.astype(jnp.bfloat16).reshape(pair_dev, 2 * sample, kv_here, HEAD)
    query = query.reshape(pair_dev, 2 * sample, kv_here, heads_here // kv_here, HEAD)
    mixed = attend(query, key_rows, value_rows, key_mask(row_lengths, sample))
    branch = jnp.dot(
        mixed, lax.all_gather(w_out, "fsdp", axis=1, tiled=True), preferred_element_type=jnp.float32
    )
    tensor_offset = lax.axis_index("tensor") * share_width
    summed_branch = lax.psum(branch.astype(jnp.bfloat16), "tensor").astype(jnp.float32)
    stream = inputs + summed_branch
    normed = rms_scale(stream, ffn_gain).astype(jnp.bfloat16)
    resid = lax.dynamic_slice_in_dim(stream, tensor_offset, share_width, 1).astype(jnp.bfloat16)
    return (
        resid.reshape(1, pair_dev, 2 * sample, share_width),
        normed.reshape(1, pair_dev, 2 * sample, width),
    )


def solution(mesh):
    return jax.shard_map(
        on_device,
        mesh=mesh,
        in_specs=(
            P("dp", "fsdp", None, "tensor"),
            P("dp", "fsdp"),
            P("dp", None, None),
            P(),
            P("fsdp", "tensor"),
            P("fsdp", "tensor"),
            P("fsdp", "tensor"),
            P("tensor", "fsdp"),
            P(),
        ),
        out_specs=(P("dp", "fsdp", None, "tensor"), P("dp", "fsdp", None, None)),
        check_vma=False,
    )
```

profile of v0, /device:TPU:1, one launch (start us, length us, event | category | flops | bytes accessed | tf_op | source)
XLA Modules:
  0.0 435.5 jit_solution(9335540852514452237)
XLA Ops:
  7.2 0.8 copy.66
  8.6 0.7 convolution_convert_fusion.2
  9.8 1.3 copy.68
  11.1 3.6 all-to-all-start
  14.9 13.6 %all-to-all-done = bf16[2,4,64,1024]{3,1,2,0:T(4,128)(2,1)S(1)} async-done(((bf16[2,4,64,1024]{3,1,2,0:T(4,128)(2,1)}), bf16[2,4,64,1024]{3,1,2,0:T(4,128)(2,1)S(1)}, u32[]{:S(2)}, u32[]{:S(2)}) %all-to-all-start) | async-done | bytes 1048608 | tf_op jit(solution)/shard_map/all_to_all | solution.py:100
  29.5 1.5 convolution_convert_fusion.1
  31.0 1.0 copy.74
  32.1 0.7 all-gather.8.cloned.1.call-update
  34.2 3.2 all-to-all-start.1
  38.3 1.6 all-to-all-done.1
  42.4 24.7 %all-gather.6.cloned.1.call-done = bf16[8,64,4096]{2,0,1:T(8,128)(2,1)} async-done(((bf16[8,64,1024]{2,0,1:T(8,128)(2,1)}), bf16[8,64,4096]{2,0,1:T(8,128)(2,1)}) %all-gather.6.cloned.1.call-update) | async-done | bytes 4194320 | tf_op jit(solution)/shard_map/all_gather | solution.py:131
  67.1 3.1 multiply_reduce_fusion.1
  70.5 3.7 multiply_convert_fusion.1
  74.3 4.3 copy.76
  78.6 2.4 copy.70
  81.1 3.2 copy-done.2
  84.3 3.5 fusion.1
  87.7 1.9 all-gather.10.cloned.1.call-done
  89.6 4.0 convolution_bitcast_fusion
  94.2 7.0 %fusion.3 = bf16[512,4096]{1,0:T(8,128)(2,1)} fusion(f32[8,64,4096]{2,1,0:T(8,128)} %copy-done.2, f32[4096]{0:T(1024)S(1)} %copy-done.5, f32[512]{0:T(512)S(1)} %rsqrt.25), kind=kLoop, calls=%fused_computation.6 | loop fusion | flops 6291456 | bytes 12601344 | tf_op jit(solution)/shard_map/convert_element_type | solution.py:135
  101.2 11.3 %all-gather.8.cloned.1.call-done = bf16[4096,128]{1,0:T(8,128)(2,1)} async-done(((bf16[2048,128]{1,0:T(8,128)(2,1)}), bf16[4096,128]{1,0:T(8,128)(2,1)}) %all-gather.8.cloned.1.call-update) | async-done | bytes 1048592 | tf_op jit(solution)/shard_map/all_gather | solution.py:150
  112.5 3.7 convolution_convert_fusion.4
  116.3 101.7 %all-gather.12.cloned.1.call-done = bf16[4096,1024]{1,0:T(8,128)(2,1)} async-done(((bf16[2048,1024]{1,0:T(8,128)(2,1)}), bf16[4096,1024]{1,0:T(8,128)(2,1)}) %all-gather.12.cloned.1.call-update) | async-done | bytes 8388624 | tf_op jit(solution)/shard_map/all_gather | solution.py:140
  218.0 12.0 %copy.77 = bf16[1024,4096]{1,0:T(8,128)(2,1)} copy(bf16[1024,4096]{0,1:T(8,128)(2,1)} %bitcast.87) | data formatting | bytes 16777216 | tf_op jit(solution)/shard_map/dot_general | solution.py:138
  230.0 8.5 %fusion.35 = f32[4,128,8,128]{1,3,2,0:T(8,128)S(1)} fusion(bf16[4,128,4096,1]{2,1,3,0:T(8,128)(2,1)} %bitcast.89, bf16[8,128,4096,1]{2,1,0,3:T(8,128)(2,1)} %bitcast.88), kind=kOutput, calls=%fused_computation.93 | convolution fusion | flops 4294967296 | bytes 14680064 | tf_op jit(solution)/shard_map/dot_general | solution.py:138
  240.3 0.7 copy.82
  241.0 82.4 %all-gather.14.cloned.1.call-done = bf16[1024,4096]{1,0:T(8,128)(2,1)} async-done(((bf16[1024,2048]{1,0:T(8,128)(2,1)}), bf16[1024,4096]{1,0:T(8,128)(2,1)}) %all-gather.14.cloned.1.call-update) | async-done | bytes 8388624 | tf_op jit(solution)/shard_map/all_gather | solution.py:166
  323.4 9.4 %convolution_convert_fusion = bf16[512,4096]{1,0:T(8,128)(2,1)} fusion(bf16[1024,4096]{1,0:T(8,128)(2,1)} %all-gather.14.cloned.1.call-done, bf16[64,8,8,128]{3,2,1,0:T(8,128)(2,1)S(1)} %bitcast.92), kind=kOutput, calls=%fused_computation.11 | convolution fusion | flops 4297064448 | bytes 13631488 | tf_op jit(solution)/shard_map/dot_general | solution.py:165
  332.8 85.5 %all-reduce.2.cloned.1.call-done = bf16[512,4096]{1,0:T(8,128)(2,1)} async-done(((bf16[512,4096]{1,0:T(8,128)(2,1)}), bf16[512,4096]{1,0:T(8,128)(2,1)}) %all-reduce.2.cloned.1.call-update) | async-done | bytes 4194320 | tf_op jit(solution)/shard_map/psum | solution.py:169
  418.3 5.8 %multiply_reduce_fusion = (f32[512]{0:T(512)S(1)}, f32[512,4096]{1,0:T(8,128)S(1)}) fusion(bf16[512,4096]{1,0:T(8,128)(2,1)} %all-reduce.2.cloned.1.call-done, f32[8,64,4096]{2,1,0:T(8,128)} %copy-done.2), kind=kLoop, calls=%fused_computation.8 | loop fusion | flops 8388096 | bytes 20973568 | tf_op jit(solution)/shard_map/reduce_sum | solution.py:14
  424.2 1.1 dynamic-slice_convert_fusion
  425.3 3.3 multiply_convert_fusion
  (64 shorter events, 9.6 us)
Async XLA Ops:
  7.2 1.4 copy-start
  11.1 17.5 %all-to-all-start = ((bf16[2,4,64,1024]{3,1,2,0:T(4,128)(2,1)}), bf16[2,4,64,1024]{3,1,2,0:T(4,128)(2,1)S(1)}, u32[]{:S(2)}, u32[]{:S(2)}) async-start(bf16[2,4,64,1024]{3,1,2,0:T(4,128)(2,1)} %copy.68), calls=%async_computation | async-start | bytes 2097152 | tf_op jit(solution)/shard_map/all_to_all | solution.py:100
  14.7 16.3 %copy-start.4 = (bf16[2048,128]{1,0:T(8,128)(2,1)S(1)}, bf16[2048,128]{1,0:T(8,128)(2,1)}, u32[]{:S(2)}) copy-start(bf16[2048,128]{1,0:T(8,128)(2,1)} %param.14) | copy-start | bytes 1572868
  14.7 52.4 %all-gather.6.cloned.1.call-start = ((), (), s32[]{:S(2)}) async-start(), calls=%async_computation.2 | async-start | bytes 5242880 | tf_op jit(solution)/shard_map/all_gather | solution.py:131
  30.9 2.5 copy-start.7
  31.0 58.7 %all-gather.10.cloned.1.call-start = ((), (), s32[]{:S(2)}) async-start(), calls=%async_computation.4 | async-start | bytes 1572864 | tf_op jit(solution)/shard_map/all_gather | solution.py:145
  32.1 80.4 %all-gather.8.cloned.1.call-start = ((), (), s32[]{:S(2)}) async-start(), calls=%async_computation.3 | async-start | bytes 1572864 | tf_op jit(solution)/shard_map/all_gather | solution.py:150
  32.8 185.1 %all-gather.12.cloned.1.call-start = ((), (), s32[]{:S(2)}) async-start(), calls=%async_computation.5 | async-start | bytes 12582912 | tf_op jit(solution)/shard_map/all_gather | solution.py:140
  34.2 5.7 %all-to-all-start.1 = ((s32[2,1,4]{2,1,0:T(1,128)}), s32[2,1,4]{2,1,0:T(1,128)S(1)}, u32[]{:S(2)}, u32[]{:S(2)}) async-start(s32[2,1,4]{2,1,0:T(1,128)} %bitcast.7), calls=%async_computation.1 | async-start | bytes 2048 | tf_op jit(solution)/shard_map/all_to_all | solution.py:107
  37.4 33.2 %copy-start.5 = (f32[4096]{0:T(1024)S(1)}, f32[4096]{0:T(1024)}, u32[]{:S(2)}) copy-start(f32[4096]{0:T(1024)} %param.12) | copy-start | bytes 49156
  37.4 286.0 %all-gather.14.cloned.1.call-start = ((), (), s32[]{:S(2)}) async-start(), calls=%async_computation.6 | async-start | bytes 12582912 | tf_op jit(solution)/shard_map/all_gather | solution.py:166
  38.0 380.3 %all-reduce.2.cloned.1.call-start = ((), (), s32[]{:S(2)}) async-start(), calls=%async_computation.7 | async-start | bytes 8388608 | tf_op jit(solution)/shard_map/psum | solution.py:169
  74.3 4.4 copy-start.3
  81.1 3.2 copy-start.2
  332.8 92.5 %copy-start.6 = (f32[4096]{0:T(1024)S(1)}, f32[4096]{0:T(1024)}, u32[]{:S(2)}) copy-start(f32[4096]{0:T(1024)} %param.17) | copy-start | bytes 49156
  424.2 4.5 %copy-start.1 = (bf16[1,8,64,1024]{3,2,1,0:T(8,128)(2,1)S(1)}, bf16[1,8,64,1024]{3,2,1,0:T(8,128)(2,1)}, u32[]{:S(2)}) copy-start(bf16[1,8,64,1024]{3,2,1,0:T(8,128)(2,1)} %param.9) | copy-start | bytes 3145732
Sparse Core Ops, SparseCore 0:
  31.1 36.0 all-gather.5
  68.7 20.9 all-gather.9
  91.2 21.2 all-gather.7
  113.9 104.0 all-gather.11
  219.4 103.9 all-gather.13
  332.9 85.3 all-reduce.1
where the time goes:
time: 437 us; the launch traced here: 436 us
  waiting for transfers between devices  325 us (74%)
  local copies, waits for them, and re-layouts  30.3 us (7%)
  other arithmetic  30.2 us (7%)
  matrix products  28.9 us (7%)
  between operations  14.4 us (3%)
  starting transfers between devices  7.2 us (2%)
    all_gather x1, waiting for transfers between devices, on_device(): lax.all_gather(w_query, 'fsdp', axis=0, tiled=True)  102 us
    psum x1, waiting for transfers between devices, on_device(): lax.psum(branch.astype(jnp.bfloat16), 'tensor').astype(jnp.float32)  85.5 us
    all_gather x1, waiting for transfers between devices, on_device(): lax.all_gather(w_out, 'fsdp', axis=1, tiled=True)  82.4 us
    all_gather x1, waiting for transfers between devices, on_device(): full_rows = lax.all_gather(local_rows, 'tensor', axis=2, tiled=True)  24.7 us
    convert_element_type x3, other arithmetic, on_device(): normal_rows = rms_scale(inputs, attn_gain).astype(jnp.bfloat16)  14.2 us
    all_to_all x1, waiting for transfers between devices, on_device(): lax.all_to_all(outgoing.reshape(fsdp_count, most_slots, sample, share_wid...  13.6 us
    dot_general x1, local copies, waits for them, and re-layouts, on_device(): jnp.dot(normal_rows, lax.all_gather(w_query, 'fsdp', axis=0, tiled=True),...  12 us
    all_gather x1, waiting for transfers between devices, on_device(): lax.all_gather(w_value, 'fsdp', axis=0, tiled=True)  11.3 us
  transfers between devices with their start and end apart: 8, of which 8 were waited for; matrix products, arithmetic and copies ran while one was open for 14% of the time, Pallas kernels for 0%

commit v1 on v0

--- a/solution.py
+++ b/solution.py
@@ -1,6 +1,9 @@
 import jax
 import jax.numpy as jnp
+import numpy as np
 from jax import lax
+from jax.experimental import pallas as pl
+from jax.experimental.pallas import tpu as pltpu
 from jax.sharding import PartitionSpec as P
 
 HEAD = 128
@@ -176,9 +179,425 @@
     )
 
 
+MESH = pl.DeviceIdType.MESH
+CH = 4
+X1, Y1, S1A, S1B, XQ, XS, XM, SB, YB, XR, YR1, YR2, SR0, SR1, SR2, SR3, LN = range(17)
+
+
+def plane_kernel(
+    pair_ref, lens_ref, gain1_ref, gain2_ref, cos_ref, sin_ref, freq_ref,
+    cand_ref, wq_ref, wk_ref, wv_ref, wo_ref,
+    resid_ref, normed_ref,
+    grid_x, relay, lhs, w_in, w_out, q_send, q_recv, q_own, ss_own, ss_recv, lens_all,
+    mix_own, mix_recv, acc_own, sib_send, sib_recv, y_send, y_recv, x_send, stream, out_rows,
+    send_sem, recv_sem, load_sem, local_sem, store_sem,
+):
+    f = lax.axis_index("fsdp")
+    t = lax.axis_index("tensor")
+    y = t // 2
+    c = t % 2
+    x_dev = {"fsdp": 1 - f}
+    t_y = (t + 2) % 4
+    t_s = t + 1 - 2 * c
+    t_sy = (t_s + 2) % 4
+    y_dev = {"tensor": t_y}
+    s_dev = {"tensor": t_s}
+    even = f == y
+
+    def remote(kind, j, src, dst, dev):
+        return pltpu.make_async_remote_copy(
+            src_ref=src, dst_ref=dst, send_sem=send_sem.at[kind, j],
+            recv_sem=recv_sem.at[kind, j], device_id=dev, device_id_type=MESH,
+        )
+
+    loads = []
+
+    def load(src, dst):
+        copy = pltpu.make_async_copy(src, dst, load_sem.at[len(loads)])
+        copy.start()
+        loads.append(copy)
+
+    mine = pl.multiple_of(f * 512, 512)
+    other = pl.multiple_of((1 - f) * 512, 512)
+    load(wq_ref.at[:, pl.ds(mine, 512)], w_in.at[:, 0:512])
+    load(wq_ref.at[:, pl.ds(other, 512)], w_in.at[:, 512:1024])
+    load(wk_ref, w_in.at[:, 1024:1152])
+    load(wv_ref, w_in.at[:, 1152:1280])
+    for r, row in enumerate((mine, other)):
+        for b, block in enumerate((t, t_y, t_s, t_sy)):
+            load(
+                wo_ref.at[pl.ds(row, 512), pl.ds(pl.multiple_of(block * 512, 512), 512)],
+                w_out.at[r * 512:(r + 1) * 512, b * 512:(b + 1) * 512],
+            )
+
+    barrier = pltpu.get_barrier_semaphore()
+    for dev in (x_dev, y_dev, s_dev):
+        pl.semaphore_signal(barrier, inc=1, device_id=dev, device_id_type=MESH)
+    pl.semaphore_wait(barrier, 3)
+
+    lens_copy = remote(LN, 0, lens_ref, lens_all.at[pl.ds(pl.multiple_of(f * 8, 8), 8)], x_dev)
+    lens_copy.start()
+    lens_all[pl.ds(pl.multiple_of(f * 8, 8), 8), :] = lens_ref[...]
+
+    cols = pl.ds(pl.multiple_of(c * 1024, 1024), 1024)
+
+    def place(g, j):
+        return grid_x.at[pl.ds(g * 8 + 2 * j, 2), :, cols]
+
+    def own(j):
+        return cand_ref.at[2 * j:2 * j + 2]
+
+    def hop(j):
+        return relay.at[2 * j:2 * j + 2]
+
+    def local_copy(j):
+        return pltpu.make_async_copy(own(j), place(f, j), local_sem.at[j])
+
+    for j in range(CH):
+
+        @pl.when(even)
+        def _():
+            remote(Y1, j, own(j), place(f, j), y_dev).start()
+            local_copy(j).start()
+
+        @pl.when(jnp.logical_not(even))
+        def _():
+            remote(Y1, j, own(j), hop(j), y_dev).start()
+            remote(X1, j, own(j), place(f, j), x_dev).start()
+
+    for copy in loads[:4]:
+        copy.wait()
+
+    def finish(j):
+        remote(XQ, j, q_send.at[j], q_recv.at[j], x_dev).wait_recv()
+        remote(XS, j, ss_own.at[j], ss_recv.at[j], x_dev).wait_recv()
+        total = (ss_own[j] + ss_recv[j])[0:1, :]
+        scale = lax.rsqrt(total * (1.0 / 4096.0) + epsilon)
+        column = jnp.broadcast_to(scale, (128, 256)).T
+        for m in range(6):
+            part = slice(m * 128, (m + 1) * 128)
+            summed = q_own[4 * j:4 * j + 4, :, part].reshape(256, 128) + q_recv[
+                j, :, part
+            ].astype(jnp.float32)
+            q_own[4 * j:4 * j + 4, :, part] = (summed * column).reshape(4, 64, 128)
+
+    for j in range(CH):
+
+        @pl.when(even)
+        def _():
+            remote(Y1, j, own(j), hop(j), y_dev).wait_recv()
+            remote(X1, j, hop(j), place(f, j), x_dev).start()
+            local_copy(j).wait()
+
+        @pl.when(jnp.logical_not(even))
+        def _():
+            remote(Y1, j, own(j), place(f, j), y_dev).wait_recv()
+
+        remote(S1A, j, place(f, j), place(f, j), s_dev).start()
+        remote(X1, j, own(j), place(1 - f, j), x_dev).wait_recv()
+        remote(S1B, j, place(1 - f, j), place(1 - f, j), s_dev).start()
+        remote(S1A, j, place(f, j), place(f, j), s_dev).wait_recv()
+        remote(S1B, j, place(1 - f, j), place(1 - f, j), s_dev).wait_recv()
+
+        gain = gain1_ref[f]
+        for g in range(2):
+            values = grid_x[g * 8 + 2 * j:g * 8 + 2 * j + 2].reshape(128, 2048).astype(jnp.float32)
+            squares = jnp.sum(values * values, axis=1, keepdims=True)
+            ss_own[j, :, g * 128:(g + 1) * 128] = jnp.broadcast_to(squares, (128, 128)).T[0:8]
+            lhs[g * 128:(g + 1) * 128, :] = (values * gain).astype(jnp.bfloat16)
+
+        def project(n):
+            return jnp.dot(
+                lhs[...],
+                w_in[:, pl.ds(pl.multiple_of(n * 256, 256), 256)],
+                preferred_element_type=jnp.float32,
+            )
+
+        @pl.loop(0, 3)
+        def _(n):
+            result = project(n + 2)
+            at = pl.ds(pl.multiple_of(n * 256, 256), 256)
+            q_send[j, :, at] = result.astype(jnp.bfloat16)
+
+        q_own[4 * j:4 * j + 4, :, 512:768] = project(4).reshape(4, 64, 256)
+        remote(XQ, j, q_send.at[j], q_recv.at[j], x_dev).start()
+        remote(XS, j, ss_own.at[j], ss_recv.at[j], x_dev).start()
+
+        @pl.loop(0, 2)
+        def _(n):
+            result = project(n)
+            at = pl.ds(pl.multiple_of(n * 256, 256), 256)
+            q_own[4 * j:4 * j + 4, :, at] = result.reshape(4, 64, 256)
+
+        if j > 0:
+            finish(j - 1)
+    finish(CH - 1)
+    lens_copy.wait()
+
+    lane = lax.broadcasted_iota(jnp.int32, (1, 128), 1)
+    sign = jnp.where(lane < 64, -1.0, 1.0)
+    slot_t = lax.broadcasted_iota(jnp.int32, (128, 128), 0)
+    slot_u = lax.broadcasted_iota(jnp.int32, (128, 128), 1)
+
+    def packed(cand):
+        return ((cand % 8) // 2) * 4 + (cand // 8) * 2 + cand % 2
+
+    def attention(k, half):
+        row = half * 4 + k
+        cand0, cand1 = pair_ref[row, 0], pair_ref[row, 1]
+        at0, at1 = packed(cand0), packed(cand1)
+        len0 = lens_all[pl.ds(cand0, 1), :]
+        len1 = lens_all[pl.ds(cand1, 1), :]
+        angle = len0.astype(jnp.float32) * freq_ref[...]
+        shift_cos, shift_sin = jnp.cos(angle), jnp.sin(angle)
+        cos0, sin0 = cos_ref[...], sin_ref[...]
+        cosine = jnp.concatenate([cos0, cos0 * shift_cos - sin0 * shift_sin], axis=0)
+        sine = jnp.concatenate([sin0, sin0 * shift_cos + cos0 * shift_sin], axis=0) * sign
+        allowed = (slot_u <= slot_t) & (lane < jnp.where(lane < 64, len0, len1 + 64))
+
+        def block(m):
+            part = slice(m * 128, (m + 1) * 128)
+            return jnp.concatenate([q_own[at0, :, part], q_own[at1, :, part]], axis=0)
+
+        def turned(m):
+            values = block(m)
+            return (values * cosine + pltpu.roll(values, 64, axis=1) * sine).astype(jnp.bfloat16)
+
+        keys = turned(4)
+        value_rows = block(5).astype(jnp.bfloat16)
+        for h in range(4):
+            scores = lax.dot_general(
+                turned(h), keys, (((1,), (1,)), ((), ())), preferred_element_type=jnp.float32
+            ) * HEAD ** (-0.5)
+            scores = jnp.where(allowed, scores, -1e30)
+            weights = jnp.exp(scores - jnp.max(scores, axis=1, keepdims=True))
+            probs = weights / jnp.sum(weights, axis=1, keepdims=True)
+            mixed = jnp.dot(
+                probs.astype(jnp.bfloat16), value_rows, preferred_element_type=jnp.float32
+            )
+            mix_own[k, half * 128:(half + 1) * 128, h * 128:(h + 1) * 128] = mixed.astype(
+                jnp.bfloat16
+            )
+
+    def stream_at(block, k):
+        return stream.at[block, k]
+
+    def own_block(k):
+        return stream_at(f * 4 + t, k)
+
+    def far_block(k):
+        return stream_at((1 - f) * 4 + t, k)
+
+    def share(kind, ref, k, dev):
+        return remote(kind, k, ref, ref, dev)
+
+    def mix_copy(k):
+        return remote(XM, k, mix_own.at[k], mix_recv.at[k], x_dev)
+
+    def partial_copy(k):
+        return remote(SB, k, sib_send.at[k], sib_recv.at[k], s_dev)
+
+    def pair_copy(k):
+        return remote(YB, k, y_send.at[k], y_recv.at[k], y_dev)
+
+    def cross_copy(k):
+        return remote(XR, k, x_send.at[k], own_block(k), x_dev)
+
+    def project_out(k):
+        mix_copy(k).wait_recv()
+
+        def term(n):
+            at = pl.ds(pl.multiple_of(n * 256, 256), 256)
+            return jnp.dot(
+                mix_own[k], w_out[0:512, at], preferred_element_type=jnp.float32
+            ) + jnp.dot(mix_recv[k], w_out[512:1024, at], preferred_element_type=jnp.float32)
+
+        @pl.loop(0, 4)
+        def _(n):
+            at = pl.ds(pl.multiple_of(n * 256, 256), 256)
+            sib_send[k, :, at] = term(n + 4).astype(jnp.bfloat16)
+
+        partial_copy(k).start()
+
+        @pl.loop(0, 4)
+        def _(n):
+            acc_own[k, :, pl.ds(pl.multiple_of(n * 256, 256), 256)] = term(n)
+
+    def add_sibling(k):
+        partial_copy(k).wait_recv()
+        y_send[k] = (acc_own[k, :, 512:] + sib_recv[k, :, 512:].astype(jnp.float32)).astype(
+            jnp.bfloat16
+        )
+        pair_copy(k).start()
+        acc_own[k, :, 0:512] = acc_own[k, :, 0:512] + sib_recv[k, :, 0:512].astype(jnp.float32)
+
+    def add_rows(k):
+        pair_copy(k).wait_recv()
+        at = pl.ds(pl.multiple_of(t * 512, 512), 512)
+        parts = []
+        for half in range(2):
+            row = half * 4 + k
+            rows = jnp.concatenate(
+                [grid_x[pair_ref[row, 0], :, at], grid_x[pair_ref[row, 1], :, at]], axis=0
+            )
+            part = slice(half * 128, (half + 1) * 128)
+            branch = acc_own[k, part, 0:512] + y_recv[k, part, :].astype(jnp.float32)
+            parts.append(rows.astype(jnp.float32) + branch)
+        first = f == 0
+        x_send[k] = jnp.where(first, parts[1], parts[0]).astype(jnp.bfloat16)
+        cross_copy(k).start()
+        stream[f * 4 + t, k] = jnp.where(first, parts[0], parts[1]).astype(jnp.bfloat16)
+        share(YR1, own_block(k), k, y_dev).start()
+        share(SR0, own_block(k), k, s_dev).start()
+
+    def pass_far(k):
+        remote(XR, k, x_send.at[k], far_block(k), x_dev).wait_recv()
+        share(YR2, far_block(k), k, y_dev).start()
+        share(SR1, far_block(k), k, s_dev).start()
+
+    def pass_pair(k):
+        near = stream_at(f * 4 + t_y, k)
+        far = stream_at((1 - f) * 4 + t_y, k)
+        share(YR1, near, k, y_dev).wait_recv()
+        share(SR2, near, k, s_dev).start()
+        share(YR2, far, k, y_dev).wait_recv()
+        share(SR3, far, k, s_dev).start()
+
+    def resid_copy(k, b):
+        return pltpu.make_async_copy(
+            stream.at[2 * t + b, k],
+            resid_ref.at[k, :, b * 512:(b + 1) * 512],
+            store_sem.at[k, b],
+        )
+
+    def normed_copy(k):
+        return pltpu.make_async_copy(out_rows.at[k], normed_ref.at[k], store_sem.at[k, 2])
+
+    def norm(k):
+        share(SR0, stream_at(f * 4 + t_s, k), k, s_dev).wait_recv()
+        share(SR1, stream_at((1 - f) * 4 + t_s, k), k, s_dev).wait_recv()
+        share(SR2, stream_at(f * 4 + t_sy, k), k, s_dev).wait_recv()
+        share(SR3, stream_at((1 - f) * 4 + t_sy, k), k, s_dev).wait_recv()
+        resid_copy(k, 0).start()
+        resid_copy(k, 1).start()
+        squares = jnp.zeros((128, 512), jnp.float32)
+        for b in range(8):
+            values = stream[b, k].astype(jnp.float32)
+            squares = squares + values * values
+        scale = lax.rsqrt(jnp.sum(squares, axis=1, keepdims=True) * (1.0 / 4096.0) + epsilon)
+        for b in range(8):
+            part = slice(b * 512, (b + 1) * 512)
+            out_rows[k, :, part] = (
+                stream[b, k].astype(jnp.float32) * scale * gain2_ref[:, part]
+            ).astype(jnp.bfloat16)
+        normed_copy(k).start()
+
+    for copy in loads[4:]:
+        copy.wait()
+    stages = (project_out, add_sibling, add_rows, pass_far, pass_pair, norm)
+    for step in range(CH + len(stages)):
+        if step < CH:
+            attention(step, 0)
+            attention(step, 1)
+            mix_copy(step).start()
+        for late in range(len(stages) - 1, -1, -1):
+            k = step - 1 - late
+            if 0 <= k < CH:
+                stages[late](k)
+
+    for j in range(CH):
+
+        @pl.when(even)
+        def _():
+            remote(Y1, j, own(j), place(f, j), y_dev).wait_send()
+            remote(X1, j, hop(j), place(f, j), x_dev).wait_send()
+
+        @pl.when(jnp.logical_not(even))
+        def _():
+            remote(Y1, j, own(j), hop(j), y_dev).wait_send()
+            remote(X1, j, own(j), place(f, j), x_dev).wait_send()
+
+        remote(S1A, j, place(f, j), place(f, j), s_dev).wait_send()
+        remote(S1B, j, place(1 - f, j), place(1 - f, j), s_dev).wait_send()
+        remote(XQ, j, q_send.at[j], q_recv.at[j], x_dev).wait_send()
+        remote(XS, j, ss_own.at[j], ss_recv.at[j], x_dev).wait_send()
+        mix_copy(j).wait_send()
+        partial_copy(j).wait_send()
+        pair_copy(j).wait_send()
+        cross_copy(j).wait_send()
+        share(YR1, own_block(j), j, y_dev).wait_send()
+        share(SR0, own_block(j), j, s_dev).wait_send()
+        share(YR2, far_block(j), j, y_dev).wait_send()
+        share(SR1, far_block(j), j, s_dev).wait_send()
+        share(SR2, stream_at(f * 4 + t_y, j), j, s_dev).wait_send()
+        share(SR3, stream_at((1 - f) * 4 + t_y, j), j, s_dev).wait_send()
+        resid_copy(j, 0).wait()
+        resid_copy(j, 1).wait()
+        normed_copy(j).wait()
+
+
+def on_plane(
+    candidates, cand_lengths, pairing, attn_gain, w_query, w_key, w_value, w_out, ffn_gain
+):
+    half = HEAD // 2
+    inv_freq = np.float32(rope_base) ** (-np.arange(half, dtype=np.float32) * 2.0 / HEAD)
+    freq = np.concatenate([inv_freq, inv_freq]).astype(np.float32)[None, :]
+    angles = (np.arange(64, dtype=np.float32)[:, None] * freq).astype(np.float64)
+    lens = jnp.broadcast_to(cand_lengths.reshape(8, 1), (8, 128))
+    bf16, f32 = jnp.bfloat16, jnp.float32
+    vmem = pl.BlockSpec(memory_space=pltpu.VMEM)
+    hbm = pl.BlockSpec(memory_space=pl.ANY)
+    resid, normed = pl.pallas_call(
+        plane_kernel,
+        out_shape=(
+            jax.ShapeDtypeStruct((4, 128, 1024), bf16),
+            jax.ShapeDtypeStruct((4, 128, 4096), bf16),
+        ),
+        in_specs=[pl.BlockSpec(memory_space=pltpu.SMEM)] + [vmem] * 6 + [hbm] * 5,
+        out_specs=(hbm, hbm),
+        scratch_shapes=[
+            pltpu.VMEM((16, 64, 2048), bf16),
+            pltpu.VMEM((8, 64, 1024), bf16),
+            pltpu.VMEM((256, 2048), bf16),
+            pltpu.VMEM((2048, 1280), bf16),
+            pltpu.VMEM((1024, 2048), bf16),
+            pltpu.VMEM((CH, 256, 768), bf16),
+            pltpu.VMEM((CH, 256, 768), bf16),
+            pltpu.VMEM((16, 64, 768), f32),
+            pltpu.VMEM((CH, 8, 256), f32),
+            pltpu.VMEM((CH, 8, 256), f32),
+            pltpu.VMEM((16, 128), jnp.int32),
+            pltpu.VMEM((CH, 256, 512), bf16),
+            pltpu.VMEM((CH, 256, 512), bf16),
+            pltpu.VMEM((CH, 256, 1024), f32),
+            pltpu.VMEM((CH, 256, 1024), bf16),
+            pltpu.VMEM((CH, 256, 1024), bf16),
+            pltpu.VMEM((CH, 256, 512), bf16),
+            pltpu.VMEM((CH, 256, 512), bf16),
+            pltpu.VMEM((CH, 128, 512), bf16),
+            pltpu.VMEM((8, CH, 128, 512), bf16),
+            pltpu.VMEM((CH, 128, 4096), bf16),
+            pltpu.SemaphoreType.DMA((17, CH)),
+            pltpu.SemaphoreType.DMA((17, CH)),
+            pltpu.SemaphoreType.DMA((12,)),
+            pltpu.SemaphoreType.DMA((CH,)),
+            pltpu.SemaphoreType.DMA((CH, 3)),
+        ],
+        compiler_params=pltpu.CompilerParams(
+            collective_id=0, has_side_effects=True, vmem_limit_bytes=58 * 2**20
+        ),
+    )(
+        pairing[0], lens, attn_gain.reshape(2, 1, 2048), ffn_gain.reshape(1, 4096),
+        jnp.asarray(np.cos(angles), f32), jnp.asarray(np.sin(angles), f32), jnp.asarray(freq),
+        candidates[0], w_query, w_key, w_value, w_out,
+    )
+    return resid[None], normed[None]
+
+
 def solution(mesh):
+    plane = mesh.shape["fsdp"] == 2 and mesh.shape["tensor"] == 4
     return jax.shard_map(
-        on_device,
+        on_plane if plane else on_device,
         mesh=mesh,
         in_specs=(
             P("dp", "fsdp", None, "tensor"),

time: 437 us -> 151 us (0.35)
  waiting for transfers between devices: 325 us -> 0 us
  Pallas kernels: 0 us -> 141 us
  other arithmetic: 30.2 us -> 0 us
  matrix products: 28.9 us -> 0 us
  local copies, waits for them, and re-layouts: 30.3 us -> 9.62 us
  between operations: 14.4 us -> 0.64 us
  starting transfers between devices: 7.2 us -> 0 us
    all_gather x5 -> x0, waiting for transfers between devices: 222 us -> none  [the longest x1 102 us: on_device(): lax.all_gather(w_query, 'fsdp', axis=0, tiled=True)]
    pallas_call x0 -> x1, Pallas kernels: none -> 141 us  [on_plane(): pl.pallas_call(plane_kernel, out_shape=(jax.ShapeDtypeStruct((4, 128, 102...]
    psum x1 -> x0, waiting for transfers between devices: 85.5 us -> none  [on_device(): lax.psum(branch.astype(jnp.bfloat16), 'tensor').astype(jnp.float32)]
    dot_general x8 -> x0, matrix products: 28.9 us -> none  [the longest x1 9.39 us: on_device(): jnp.dot(mixed, lax.all_gather(w_out, 'fsdp', axis=1, tiled=True), preferr...]
    convert_element_type x5 -> x0, other arithmetic: 17.6 us -> none  [the longest x3 14.2 us: on_device(): normal_rows = rms_scale(inputs, attn_gain).astype(jnp.bfloat16)]
    all_to_all x2 -> x0, waiting for transfers between devices: 15.3 us -> none  [the longest x1 13.6 us: on_device(): lax.all_to_all(outgoing.reshape(fsdp_count, most_slots, sample, share_wid...]
    dot_general x1 -> x0, local copies, waits for them, and re-layouts: 12 us -> none  [on_device(): jnp.dot(normal_rows, lax.all_gather(w_query, 'fsdp', axis=0, tiled=True),...]
    reduce_sum x9 -> x0, other arithmetic: 10.2 us -> none  [the longest x2 8.91 us: rms_scale(): mean_square = jnp.mean(values * values, axis=-1, keepdims=True)]
  transfers between devices with their start and end apart: 8 -> 0, of which waited for: 8 -> 0; matrix products, arithmetic and copies ran while one was open for 14% -> 0% of each run, Pallas kernels for 0% -> 0%
where the time goes in v1:
time: 151 us
  Pallas kernels  141 us (93%)
  local copies, waits for them, and re-layouts  9.62 us (6%)
    pallas_call x1, Pallas kernels, on_plane(): pl.pallas_call(plane_kernel, out_shape=(jax.ShapeDtypeStruct((4, 128, 102...  141 us
    unnamed x2, local copies, waits for them, and re-layouts  6.96 us

profile of v1, /device:TPU:1, one launch (start us, length us, event | category | flops | bytes accessed | tf_op | source)
XLA Modules:
  0.0 151.1 jit_solution(559633643232532626)
XLA Ops:
  0.6 1.3 broadcast_in_dim.14.lens_ref
  1.9 1.3 copy.14.pair_ref
  3.3 140.8 %shard_map.131 = (bf16[4,128,1024]{2,1,0:T(8,128)(2,1)}, bf16[4,128,4096]{2,1,0:T(8,128)(2,1)}) custom-call(s32[8,2]{1,0:T(8,128)} %copy.14.pair_ref, s32[8,128]{1,0:T(8,128)} %broadcast_in_dim.14.lens_ref, f32[2,1,2048]{2,1,0:T(1,128)} %bitcast.10, f32[1,4096]{1,0:T(1,128)} %bitcast.11, f32[64,128]{1,0:T(8,128)} %constant.6.clone.cos_ref, ...), custom_call_target="tpu_custom_call" | custom-call | tf_op jit(solution)/shard_map/pallas_call | solution.py:550
  144.1 2.3 %copy.17 = bf16[1,4,128,1024]{3,2,1,0:T(8,128)(2,1)} copy(bf16[1,4,128,1024]{3,2,1,0:T(8,128)(2,1)} %bitcast.9) | data formatting | bytes 2097152
  146.4 4.7 %copy.18 = bf16[1,4,128,4096]{3,2,1,0:T(8,128)(2,1)} copy(bf16[1,4,128,4096]{3,2,1,0:T(8,128)(2,1)} %bitcast.7) | data formatting | bytes 8388608

commit v2 on v1

--- a/solution.py
+++ b/solution.py
@@ -181,15 +181,16 @@
 
 MESH = pl.DeviceIdType.MESH
 CH = 4
-X1, Y1, S1A, S1B, XQ, XS, XM, SB, YB, XR, YR1, YR2, SR0, SR1, SR2, SR3, LN = range(17)
+X1, Y1, Y2, S1A, S1B, S1C, XQ, XS, XM, SB, YB, XR, YR1, YR2, SR0, SR1, SR2, SR3, LN = range(19)
+KINDS = 19
 
 
 def plane_kernel(
-    pair_ref, lens_ref, gain1_ref, gain2_ref, cos_ref, sin_ref, freq_ref,
+    pair_ref, lens_ref, gain1_ref, cos_ref, sin_ref, freq_ref,
     cand_ref, wq_ref, wk_ref, wv_ref, wo_ref,
-    resid_ref, normed_ref,
-    grid_x, relay, lhs, w_in, w_out, q_send, q_recv, q_own, ss_own, ss_recv, lens_all,
-    mix_own, mix_recv, acc_own, sib_send, sib_recv, y_send, y_recv, x_send, stream, out_rows,
+    stream_ref,
+    grid_x, relay, lhs, w_in, w_out, q_send, q_recv, q_own, ss_own, ss_recv, own_lens, lens_all,
+    mix_own, mix_recv, acc_own, sib_send, sib_recv, y_send, y_recv, x_send, stream,
     send_sem, recv_sem, load_sem, local_sem, store_sem,
 ):
     f = lax.axis_index("fsdp")
@@ -235,35 +236,93 @@
         pl.semaphore_signal(barrier, inc=1, device_id=dev, device_id_type=MESH)
     pl.semaphore_wait(barrier, 3)
 
-    lens_copy = remote(LN, 0, lens_ref, lens_all.at[pl.ds(pl.multiple_of(f * 8, 8), 8)], x_dev)
+    spread = jnp.broadcast_to(lens_ref[...].astype(jnp.float32), (8, 8))
+    pick = lax.broadcasted_iota(jnp.int32, (8, 8), 0) == lax.broadcasted_iota(jnp.int32, (8, 8), 1)
+    column = jnp.sum(jnp.where(pick, spread, 0.0), axis=1, keepdims=True)
+    own_lens[...] = jnp.broadcast_to(column, (8, 128)).astype(jnp.int32)
+    lens_copy = remote(LN, 0, own_lens, lens_all.at[pl.ds(pl.multiple_of(f * 8, 8), 8)], x_dev)
     lens_copy.start()
-    lens_all[pl.ds(pl.multiple_of(f * 8, 8), 8), :] = lens_ref[...]
+    lens_all[pl.ds(pl.multiple_of(f * 8, 8), 8), :] = own_lens[...]
 
     cols = pl.ds(pl.multiple_of(c * 1024, 1024), 1024)
 
-    def place(g, j):
-        return grid_x.at[pl.ds(g * 8 + 2 * j, 2), :, cols]
-
-    def own(j):
-        return cand_ref.at[2 * j:2 * j + 2]
+    def place(g, j, at=0, count=2):
+        return grid_x.at[pl.ds(g * 8 + 2 * j + at, count), :, cols]
+
+    def own(j, at=0, count=2):
+        return cand_ref.at[2 * j + at:2 * j + at + count]
 
     def hop(j):
-        return relay.at[2 * j:2 * j + 2]
+        return relay.at[j:j + 1]
 
     def local_copy(j):
         return pltpu.make_async_copy(own(j), place(f, j), local_sem.at[j])
 
-    for j in range(CH):
-
+    def send_y(j):
         @pl.when(even)
         def _():
             remote(Y1, j, own(j), place(f, j), y_dev).start()
+
+        @pl.when(jnp.logical_not(even))
+        def _():
+            remote(Y1, j, own(j, 1, 1), hop(j), y_dev).start()
+
+    def far_x(j, at):
+        return place(1 - f, j, at, 1)
+
+    def forward_x(j):
+        @pl.when(even)
+        def _():
+            remote(Y1, j, own(j, 1, 1), hop(j), y_dev).wait_recv()
+            remote(X1, j, hop(j), place(f, j, 1, 1), x_dev).start()
+
+    def forward_y(j):
+        @pl.when(even)
+        def _():
+            remote(X1, j, own(j, 0, 1), far_x(j, 0), x_dev).wait_recv()
+            remote(Y2, j, far_x(j, 0), far_x(j, 0), y_dev).start()
+            remote(S1B, j, far_x(j, 0), far_x(j, 0), s_dev).start()
+            local_copy(j).wait()
+
+        @pl.when(jnp.logical_not(even))
+        def _():
+            remote(X1, j, hop(j), far_x(j, 1), x_dev).wait_recv()
+            remote(Y2, j, far_x(j, 1), far_x(j, 1), y_dev).start()
+            remote(S1B, j, far_x(j, 1), far_x(j, 1), s_dev).start()
+            remote(Y1, j, own(j), place(f, j), y_dev).wait_recv()
+
+        remote(S1A, j, place(f, j), place(f, j), s_dev).start()
+
+    def finish_input(j):
+        def last(at):
+            remote(Y2, j, far_x(j, at), far_x(j, at), y_dev).wait_recv()
+            remote(S1C, j, far_x(j, at), far_x(j, at), s_dev).start()
+            remote(S1B, j, far_x(j, 1 - at), far_x(j, 1 - at), s_dev).wait_recv()
+            remote(S1C, j, far_x(j, at), far_x(j, at), s_dev).wait_recv()
+
+        @pl.when(even)
+        def _():
+            last(1)
+
+        @pl.when(jnp.logical_not(even))
+        def _():
+            last(0)
+
+        remote(S1A, j, place(f, j), place(f, j), s_dev).wait_recv()
+
+    send_y(0)
+
+    @pl.when(jnp.logical_not(even))
+    def _():
+        for j in range(CH):
+            remote(X1, j, own(j, 0, 1), place(f, j, 0, 1), x_dev).start()
+
+    send_y(1)
+
+    @pl.when(even)
+    def _():
+        for j in range(CH):
             local_copy(j).start()
-
-        @pl.when(jnp.logical_not(even))
-        def _():
-            remote(Y1, j, own(j), hop(j), y_dev).start()
-            remote(X1, j, own(j), place(f, j), x_dev).start()
 
     for copy in loads[:4]:
         copy.wait()
@@ -281,23 +340,14 @@
             ].astype(jnp.float32)
             q_own[4 * j:4 * j + 4, :, part] = (summed * column).reshape(4, 64, 128)
 
+    forward_x(0)
     for j in range(CH):
-
-        @pl.when(even)
-        def _():
-            remote(Y1, j, own(j), hop(j), y_dev).wait_recv()
-            remote(X1, j, hop(j), place(f, j), x_dev).start()
-            local_copy(j).wait()
-
-        @pl.when(jnp.logical_not(even))
-        def _():
-            remote(Y1, j, own(j), place(f, j), y_dev).wait_recv()
-
-        remote(S1A, j, place(f, j), place(f, j), s_dev).start()
-        remote(X1, j, own(j), place(1 - f, j), x_dev).wait_recv()
-        remote(S1B, j, place(1 - f, j), place(1 - f, j), s_dev).start()
-        remote(S1A, j, place(f, j), place(f, j), s_dev).wait_recv()
-        remote(S1B, j, place(1 - f, j), place(1 - f, j), s_dev).wait_recv()
+        forward_y(j)
+        if j + 1 < CH:
+            forward_x(j + 1)
+        if j + 2 < CH:
+            send_y(j + 2)
+        finish_input(j)
 
         gain = gain1_ref[f]
         for g in range(2):
@@ -329,8 +379,9 @@
             at = pl.ds(pl.multiple_of(n * 256, 256), 256)
             q_own[4 * j:4 * j + 4, :, at] = result.reshape(4, 64, 256)
 
-        if j > 0:
-            finish(j - 1)
+        if j > 1:
+            finish(j - 2)
+    finish(CH - 2)
     finish(CH - 1)
     lens_copy.wait()
 
@@ -463,62 +514,71 @@
         share(YR2, far, k, y_dev).wait_recv()
         share(SR3, far, k, s_dev).start()
 
-    def resid_copy(k, b):
-        return pltpu.make_async_copy(
-            stream.at[2 * t + b, k],
-            resid_ref.at[k, :, b * 512:(b + 1) * 512],
-            store_sem.at[k, b],
-        )
-
-    def normed_copy(k):
-        return pltpu.make_async_copy(out_rows.at[k], normed_ref.at[k], store_sem.at[k, 2])
-
-    def norm(k):
+    def store_copy(k):
+        return pltpu.make_async_copy(stream.at[:, k], stream_ref.at[:, k], store_sem.at[k])
+
+    def store(k):
         share(SR0, stream_at(f * 4 + t_s, k), k, s_dev).wait_recv()
         share(SR1, stream_at((1 - f) * 4 + t_s, k), k, s_dev).wait_recv()
         share(SR2, stream_at(f * 4 + t_sy, k), k, s_dev).wait_recv()
         share(SR3, stream_at((1 - f) * 4 + t_sy, k), k, s_dev).wait_recv()
-        resid_copy(k, 0).start()
-        resid_copy(k, 1).start()
-        squares = jnp.zeros((128, 512), jnp.float32)
-        for b in range(8):
-            values = stream[b, k].astype(jnp.float32)
-            squares = squares + values * values
-        scale = lax.rsqrt(jnp.sum(squares, axis=1, keepdims=True) * (1.0 / 4096.0) + epsilon)
-        for b in range(8):
-            part = slice(b * 512, (b + 1) * 512)
-            out_rows[k, :, part] = (
-                stream[b, k].astype(jnp.float32) * scale * gain2_ref[:, part]
-            ).astype(jnp.bfloat16)
-        normed_copy(k).start()
+        store_copy(k).start()
 
     for copy in loads[4:]:
         copy.wait()
-    stages = (project_out, add_sibling, add_rows, pass_far, pass_pair, norm)
-    for step in range(CH + len(stages)):
-        if step < CH:
-            attention(step, 0)
-            attention(step, 1)
-            mix_copy(step).start()
-        for late in range(len(stages) - 1, -1, -1):
-            k = step - 1 - late
-            if 0 <= k < CH:
-                stages[late](k)
+    def attend_rows(k):
+        attention(k, 0)
+        attention(k, 1)
+        mix_copy(k).start()
+
+    attend_rows(0)
+    attend_rows(1)
+    attend_rows(2)
+    project_out(0)
+    attend_rows(3)
+    add_sibling(0)
+    project_out(1)
+    add_sibling(1)
+    add_rows(0)
+    project_out(2)
+    add_sibling(2)
+    add_rows(1)
+    pass_far(0)
+    project_out(3)
+    add_sibling(3)
+    add_rows(2)
+    pass_far(1)
+    pass_pair(0)
+    add_rows(3)
+    pass_far(2)
+    pass_pair(1)
+    store(0)
+    pass_far(3)
+    pass_pair(2)
+    store(1)
+    pass_pair(3)
+    store(2)
+    store(3)
 
     for j in range(CH):
 
         @pl.when(even)
         def _():
             remote(Y1, j, own(j), place(f, j), y_dev).wait_send()
-            remote(X1, j, hop(j), place(f, j), x_dev).wait_send()
+            remote(X1, j, hop(j), place(f, j, 1, 1), x_dev).wait_send()
+            remote(Y2, j, far_x(j, 0), far_x(j, 0), y_dev).wait_send()
+            remote(S1B, j, far_x(j, 0), far_x(j, 0), s_dev).wait_send()
+            remote(S1C, j, far_x(j, 1), far_x(j, 1), s_dev).wait_send()
 
         @pl.when(jnp.logical_not(even))
         def _():
-            remote(Y1, j, own(j), hop(j), y_dev).wait_send()
-            remote(X1, j, own(j), place(f, j), x_dev).wait_send()
+            remote(Y1, j, own(j, 1, 1), hop(j), y_dev).wait_send()
+            remote(X1, j, own(j, 0, 1), place(f, j, 0, 1), x_dev).wait_send()
+            remote(Y2, j, far_x(j, 1), far_x(j, 1), y_dev).wait_send()
+            remote(S1B, j, far_x(j, 1), far_x(j, 1), s_dev).wait_send()
+            remote(S1C, j, far_x(j, 0), far_x(j, 0), s_dev).wait_send()
 
         remote(S1A, j, place(f, j), place(f, j), s_dev).wait_send()
-        remote(S1B, j, place(1 - f, j), place(1 - f, j), s_dev).wait_send()
         remote(XQ, j, q_send.at[j], q_recv.at[j], x_dev).wait_send()
         remote(XS, j, ss_own.at[j], ss_recv.at[j], x_dev).wait_send()
         mix_copy(j).wait_send()
@@ -531,9 +591,23 @@
         share(SR1, far_block(j), j, s_dev).wait_send()
         share(SR2, stream_at(f * 4 + t_y, j), j, s_dev).wait_send()
         share(SR3, stream_at((1 - f) * 4 + t_y, j), j, s_dev).wait_send()
-        resid_copy(j, 0).wait()
-        resid_copy(j, 1).wait()
-        normed_copy(j).wait()
+        store_copy(j).wait()
+
+
+def norm_kernel(stream_ref, gain2_ref, resid_ref, normed_ref):
+    t = lax.axis_index("tensor")
+    squares = jnp.zeros((128, 512), jnp.float32)
+    for b in range(8):
+        values = stream_ref[b, 0].astype(jnp.float32)
+        squares = squares + values * values
+    scale = lax.rsqrt(jnp.sum(squares, axis=1, keepdims=True) * (1.0 / 4096.0) + epsilon)
+    for b in range(8):
+        part = slice(b * 512, (b + 1) * 512)
+        normed_ref[0, :, part] = (
+            stream_ref[b, 0].astype(jnp.float32) * scale * gain2_ref[:, part]
+        ).astype(jnp.bfloat16)
+    resid_ref[0, :, 0:512] = stream_ref[2 * t, 0]
+    resid_ref[0, :, 512:1024] = stream_ref[2 * t + 1, 0]
 
 
 def on_plane(
@@ -543,21 +617,17 @@
     inv_freq = np.float32(rope_base) ** (-np.arange(half, dtype=np.float32) * 2.0 / HEAD)
     freq = np.concatenate([inv_freq, inv_freq]).astype(np.float32)[None, :]
     angles = (np.arange(64, dtype=np.float32)[:, None] * freq).astype(np.float64)
-    lens = jnp.broadcast_to(cand_lengths.reshape(8, 1), (8, 128))
     bf16, f32 = jnp.bfloat16, jnp.float32
     vmem = pl.BlockSpec(memory_space=pltpu.VMEM)
     hbm = pl.BlockSpec(memory_space=pl.ANY)
-    resid, normed = pl.pallas_call(
+    stream = pl.pallas_call(
         plane_kernel,
-        out_shape=(
-            jax.ShapeDtypeStruct((4, 128, 1024), bf16),
-            jax.ShapeDtypeStruct((4, 128, 4096), bf16),
-        ),
-        in_specs=[pl.BlockSpec(memory_space=pltpu.SMEM)] + [vmem] * 6 + [hbm] * 5,
-        out_specs=(hbm, hbm),
+        out_shape=jax.ShapeDtypeStruct((8, CH, 128, 512), bf16),
+        in_specs=[pl.BlockSpec(memory_space=pltpu.SMEM)] + [vmem] * 5 + [hbm] * 5,
+        out_specs=hbm,
         scratch_shapes=[
             pltpu.VMEM((16, 64, 2048), bf16),
-            pltpu.VMEM((8, 64, 1024), bf16),
+            pltpu.VMEM((CH, 64, 1024), bf16),
             pltpu.VMEM((256, 2048), bf16),
             pltpu.VMEM((2048, 1280), bf16),
             pltpu.VMEM((1024, 2048), bf16),
@@ -566,6 +636,7 @@
             pltpu.VMEM((16, 64, 768), f32),
             pltpu.VMEM((CH, 8, 256), f32),
             pltpu.VMEM((CH, 8, 256), f32),
+            pltpu.VMEM((8, 128), jnp.int32),
             pltpu.VMEM((16, 128), jnp.int32),
             pltpu.VMEM((CH, 256, 512), bf16),
             pltpu.VMEM((CH, 256, 512), bf16),
@@ -576,21 +647,37 @@
             pltpu.VMEM((CH, 256, 512), bf16),
             pltpu.VMEM((CH, 128, 512), bf16),
             pltpu.VMEM((8, CH, 128, 512), bf16),
-            pltpu.VMEM((CH, 128, 4096), bf16),
-            pltpu.SemaphoreType.DMA((17, CH)),
-            pltpu.SemaphoreType.DMA((17, CH)),
+            pltpu.SemaphoreType.DMA((KINDS, CH)),
+            pltpu.SemaphoreType.DMA((KINDS, CH)),
             pltpu.SemaphoreType.DMA((12,)),
             pltpu.SemaphoreType.DMA((CH,)),
-            pltpu.SemaphoreType.DMA((CH, 3)),
+            pltpu.SemaphoreType.DMA((CH,)),
         ],
         compiler_params=pltpu.CompilerParams(
             collective_id=0, has_side_effects=True, vmem_limit_bytes=58 * 2**20
         ),
     )(
-        pairing[0], lens, attn_gain.reshape(2, 1, 2048), ffn_gain.reshape(1, 4096),
+        pairing[0], cand_lengths, attn_gain.reshape(2, 1, 2048),
         jnp.asarray(np.cos(angles), f32), jnp.asarray(np.sin(angles), f32), jnp.asarray(freq),
         candidates[0], w_query, w_key, w_value, w_out,
     )
+    resid, normed = pl.pallas_call(
+        norm_kernel,
+        grid=(CH,),
+        out_shape=(
+            jax.ShapeDtypeStruct((CH, 128, 1024), bf16),
+            jax.ShapeDtypeStruct((CH, 128, 4096), bf16),
+        ),
+        in_specs=[
+            pl.BlockSpec((8, 1, 128, 512), lambda k: (0, k, 0, 0)),
+            pl.BlockSpec((1, 4096), lambda k: (0, 0)),
+        ],
+        out_specs=(
+            pl.BlockSpec((1, 128, 1024), lambda k: (k, 0, 0)),
+            pl.BlockSpec((1, 128, 4096), lambda k: (k, 0, 0)),
+        ),
+        compiler_params=pltpu.CompilerParams(vmem_limit_bytes=32 * 2**20),
+    )(stream, ffn_gain.reshape(1, 4096))
     return resid[None], normed[None]
 
 

time: 151 us -> 137 us (0.907)
  Pallas kernels: 141 us -> 133 us
  local copies, waits for them, and re-layouts: 9.62 us -> 3.53 us
    pallas_call x1 -> x2, Pallas kernels: 141 us -> 133 us  [the longest x1 129 us: on_plane(): pl.pallas_call(plane_kernel, out_shape=jax.ShapeDtypeStruct((8, CH, 128,...]
    unnamed x2 -> x4, local copies, waits for them, and re-layouts: 6.96 us -> 2.18 us
where the time goes in v2:
time: 137 us
  Pallas kernels  133 us (97%)
  local copies, waits for them, and re-layouts  3.53 us (3%)
    pallas_call x1, Pallas kernels, on_plane(): pl.pallas_call(plane_kernel, out_shape=jax.ShapeDtypeStruct((8, CH, 128,...  129 us
    pallas_call x1, Pallas kernels, on_plane(): pl.pallas_call(norm_kernel, grid=(CH,), out_shape=(jax.ShapeDtypeStruct((...  3.64 us

profile of v2, /device:TPU:1, one launch (start us, length us, event | category | flops | bytes accessed | tf_op | source)
XLA Modules:
  0.0 136.8 jit_solution(11353988073941545879)
XLA Ops:
  0.6 1.3 copy.14.pair_ref
  2.0 0.0 copy-start.1
  2.0 129.0 %shard_map.131.stream_ref = bf16[8,4,128,512]{3,2,1,0:T(8,128)(2,1)} custom-call(s32[8,2]{1,0:T(8,128)} %copy.14.pair_ref, s32[1,8]{1,0:T(1,128)} %lens_ref.1, f32[2,1,2048]{2,1,0:T(1,128)} %bitcast.8, f32[64,128]{1,0:T(8,128)} %constant.6.clone.cos_ref, f32[64,128]{1,0:T(8,128)} %constant.7.clone.sin_ref, f32[1,128]{1,0:T(1,128)} %constant.8.clone.freq_ref, ...), custom_call_target="tpu_custom_call" | custom-call | tf_op jit(solution)/shard_map/pallas_call | solution.py:623
  131.0 0.0 copy-done.1
  131.0 0.0 copy-start
  131.0 2.2 %copy-done = bf16[8,4,128,512]{3,2,1,0:T(8,128)(2,1)S(1)} copy-done((bf16[8,4,128,512]{3,2,1,0:T(8,128)(2,1)S(1)}, bf16[8,4,128,512]{3,2,1,0:T(8,128)(2,1)}, u32[]{:S(2)}) %copy-start) | copy-done | bytes 4194328
  133.2 3.6 %shard_map.132 = (bf16[4,128,1024]{2,1,0:T(8,128)(2,1)}, bf16[4,128,4096]{2,1,0:T(8,128)(2,1)}) custom-call(bf16[8,4,128,512]{3,2,1,0:T(8,128)(2,1)S(1)} %copy-done, f32[1,4096]{1,0:T(1,128)S(1)} %bitcast.6), custom_call_target="tpu_custom_call" | custom-call | tf_op jit(solution)/shard_map/pallas_call | solution.py:664
Async XLA Ops:
  2.0 129.0 %copy-start.1 = (f32[4096]{0:T(1024)S(1)}, f32[4096]{0:T(1024)}, u32[]{:S(2)}) copy-start(f32[4096]{0:T(1024)} %param.20) | copy-start | bytes 49156
  131.0 2.2 %copy-start = (bf16[8,4,128,512]{3,2,1,0:T(8,128)(2,1)S(1)}, bf16[8,4,128,512]{3,2,1,0:T(8,128)(2,1)}, u32[]{:S(2)}) copy-start(bf16[8,4,128,512]{3,2,1,0:T(8,128)(2,1)} %shard_map.131.stream_ref) | copy-start | bytes 12582916

commit v3 on v2

--- a/solution.py
+++ b/solution.py
@@ -181,6 +181,7 @@
 
 MESH = pl.DeviceIdType.MESH
 CH = 4
+PARTS = 8
 X1, Y1, Y2, S1A, S1B, S1C, XQ, XS, XM, SB, YB, XR, YR1, YR2, SR0, SR1, SR2, SR3, LN = range(19)
 KINDS = 19
 
@@ -416,19 +417,21 @@
 
         keys = turned(4)
         value_rows = block(5).astype(jnp.bfloat16)
+        queries = jnp.concatenate([turned(h) for h in range(4)], axis=0)
+        scores = lax.dot_general(
+            queries, keys, (((1,), (1,)), ((), ())), preferred_element_type=jnp.float32
+        ) * HEAD ** (-0.5)
+        scores = jnp.where(jnp.concatenate([allowed] * 4, axis=0), scores, -1e30)
+        weights = jnp.exp(scores - jnp.max(scores, axis=1, keepdims=True))
+        probs = weights * (1.0 / jnp.sum(weights, axis=1, keepdims=True))
+        mixed = jnp.dot(
+            probs.astype(jnp.bfloat16), value_rows, preferred_element_type=jnp.float32
+        ).astype(jnp.bfloat16)
         for h in range(4):
-            scores = lax.dot_general(
-                turned(h), keys, (((1,), (1,)), ((), ())), preferred_element_type=jnp.float32
-            ) * HEAD ** (-0.5)
-            scores = jnp.where(allowed, scores, -1e30)
-            weights = jnp.exp(scores - jnp.max(scores, axis=1, keepdims=True))
-            probs = weights / jnp.sum(weights, axis=1, keepdims=True)
-            mixed = jnp.dot(
-                probs.astype(jnp.bfloat16), value_rows, preferred_element_type=jnp.float32
-            )
-            mix_own[k, half * 128:(half + 1) * 128, h * 128:(h + 1) * 128] = mixed.astype(
-                jnp.bfloat16
-            )
+            for s in range(2):
+                mix_own[2 * k + s, half * 64:(half + 1) * 64, h * 128:(h + 1) * 128] = mixed[
+                    h * 128 + s * 64:h * 128 + (s + 1) * 64
+                ]
 
     def stream_at(block, k):
         return stream.at[block, k]
@@ -487,11 +490,8 @@
         at = pl.ds(pl.multiple_of(t * 512, 512), 512)
         parts = []
         for half in range(2):
-            row = half * 4 + k
-            rows = jnp.concatenate(
-                [grid_x[pair_ref[row, 0], :, at], grid_x[pair_ref[row, 1], :, at]], axis=0
-            )
-            part = slice(half * 128, (half + 1) * 128)
+            rows = grid_x[pair_ref[half * 4 + k // 2, k % 2], :, at]
+            part = slice(half * 64, (half + 1) * 64)
             branch = acc_own[k, part, 0:512] + y_recv[k, part, :].astype(jnp.float32)
             parts.append(rows.astype(jnp.float32) + branch)
         first = f == 0
@@ -529,36 +529,17 @@
     def attend_rows(k):
         attention(k, 0)
         attention(k, 1)
-        mix_copy(k).start()
-
-    attend_rows(0)
-    attend_rows(1)
-    attend_rows(2)
-    project_out(0)
-    attend_rows(3)
-    add_sibling(0)
-    project_out(1)
-    add_sibling(1)
-    add_rows(0)
-    project_out(2)
-    add_sibling(2)
-    add_rows(1)
-    pass_far(0)
-    project_out(3)
-    add_sibling(3)
-    add_rows(2)
-    pass_far(1)
-    pass_pair(0)
-    add_rows(3)
-    pass_far(2)
-    pass_pair(1)
-    store(0)
-    pass_far(3)
-    pass_pair(2)
-    store(1)
-    pass_pair(3)
-    store(2)
-    store(3)
+        mix_copy(2 * k).start()
+        mix_copy(2 * k + 1).start()
+
+    order = [(2.0 * j - 2.5, attend_rows, j) for j in range(PARTS // 2)]
+    for lag, stage in (
+        (0.0, project_out), (0.8, add_sibling), (2.1, add_rows),
+        (3.2, pass_far), (4.3, pass_pair), (5.4, store),
+    ):
+        order += [(k + lag, stage, k) for k in range(PARTS)]
+    for _, stage, k in sorted(order, key=lambda item: item[0]):
+        stage(k)
 
     for j in range(CH):
 
@@ -581,6 +562,7 @@
         remote(S1A, j, place(f, j), place(f, j), s_dev).wait_send()
         remote(XQ, j, q_send.at[j], q_recv.at[j], x_dev).wait_send()
         remote(XS, j, ss_own.at[j], ss_recv.at[j], x_dev).wait_send()
+    for j in range(PARTS):
         mix_copy(j).wait_send()
         partial_copy(j).wait_send()
         pair_copy(j).wait_send()
@@ -598,16 +580,16 @@
     t = lax.axis_index("tensor")
     squares = jnp.zeros((128, 512), jnp.float32)
     for b in range(8):
-        values = stream_ref[b, 0].astype(jnp.float32)
+        values = stream_ref[b].reshape(128, 512).astype(jnp.float32)
         squares = squares + values * values
     scale = lax.rsqrt(jnp.sum(squares, axis=1, keepdims=True) * (1.0 / 4096.0) + epsilon)
     for b in range(8):
         part = slice(b * 512, (b + 1) * 512)
         normed_ref[0, :, part] = (
-            stream_ref[b, 0].astype(jnp.float32) * scale * gain2_ref[:, part]
+            stream_ref[b].reshape(128, 512).astype(jnp.float32) * scale * gain2_ref[:, part]
         ).astype(jnp.bfloat16)
-    resid_ref[0, :, 0:512] = stream_ref[2 * t, 0]
-    resid_ref[0, :, 512:1024] = stream_ref[2 * t + 1, 0]
+    resid_ref[0, :, 0:512] = stream_ref[2 * t].reshape(128, 512)
+    resid_ref[0, :, 512:1024] = stream_ref[2 * t + 1].reshape(128, 512)
 
 
 def on_plane(
@@ -622,7 +604,7 @@
     hbm = pl.BlockSpec(memory_space=pl.ANY)
     stream = pl.pallas_call(
         plane_kernel,
-        out_shape=jax.ShapeDtypeStruct((8, CH, 128, 512), bf16),
+        out_shape=jax.ShapeDtypeStruct((8, PARTS, 64, 512), bf16),
         in_specs=[pl.BlockSpec(memory_space=pltpu.SMEM)] + [vmem] * 5 + [hbm] * 5,
         out_specs=hbm,
         scratch_shapes=[
@@ -638,20 +620,20 @@
             pltpu.VMEM((CH, 8, 256), f32),
             pltpu.VMEM((8, 128), jnp.int32),
             pltpu.VMEM((16, 128), jnp.int32),
-            pltpu.VMEM((CH, 256, 512), bf16),
-            pltpu.VMEM((CH, 256, 512), bf16),
-            pltpu.VMEM((CH, 256, 1024), f32),
-            pltpu.VMEM((CH, 256, 1024), bf16),
-            pltpu.VMEM((CH, 256, 1024), bf16),
-            pltpu.VMEM((CH, 256, 512), bf16),
-            pltpu.VMEM((CH, 256, 512), bf16),
-            pltpu.VMEM((CH, 128, 512), bf16),
-            pltpu.VMEM((8, CH, 128, 512), bf16),
-            pltpu.SemaphoreType.DMA((KINDS, CH)),
-            pltpu.SemaphoreType.DMA((KINDS, CH)),
+            pltpu.VMEM((PARTS, 128, 512), bf16),
+            pltpu.VMEM((PARTS, 128, 512), bf16),
+            pltpu.VMEM((PARTS, 128, 1024), f32),
+            pltpu.VMEM((PARTS, 128, 1024), bf16),
+            pltpu.VMEM((PARTS, 128, 1024), bf16),
+            pltpu.VMEM((PARTS, 128, 512), bf16),
+            pltpu.VMEM((PARTS, 128, 512), bf16),
+            pltpu.VMEM((PARTS, 64, 512), bf16),
+            pltpu.VMEM((8, PARTS, 64, 512), bf16),
+            pltpu.SemaphoreType.DMA((KINDS, PARTS)),
+            pltpu.SemaphoreType.DMA((KINDS, PARTS)),
             pltpu.SemaphoreType.DMA((12,)),
             pltpu.SemaphoreType.DMA((CH,)),
-            pltpu.SemaphoreType.DMA((CH,)),
+            pltpu.SemaphoreType.DMA((PARTS,)),
         ],
         compiler_params=pltpu.CompilerParams(
             collective_id=0, has_side_effects=True, vmem_limit_bytes=58 * 2**20
@@ -669,14 +651,14 @@
             jax.ShapeDtypeStruct((CH, 128, 4096), bf16),
         ),
         in_specs=[
-            pl.BlockSpec((8, 1, 128, 512), lambda k: (0, k, 0, 0)),
+            pl.BlockSpec((8, 2, 64, 512), lambda k: (0, k, 0, 0)),
             pl.BlockSpec((1, 4096), lambda k: (0, 0)),
         ],
         out_specs=(
             pl.BlockSpec((1, 128, 1024), lambda k: (k, 0, 0)),
             pl.BlockSpec((1, 128, 4096), lambda k: (k, 0, 0)),
         ),
-        compiler_params=pltpu.CompilerParams(vmem_limit_bytes=32 * 2**20),
+        compiler_params=pltpu.CompilerParams(vmem_limit_bytes=60 * 2**20),
     )(stream, ffn_gain.reshape(1, 4096))
     return resid[None], normed[None]
 

time: 137 us -> 134 us (0.978)
  local copies, waits for them, and re-layouts: 3.53 us -> 1.35 us
    pallas_call x1, Pallas kernels: 129 us -> 126 us  [on_plane(): pl.pallas_call(plane_kernel, out_shape=jax.ShapeDtypeStruct((8, PARTS, 64...]
    unnamed x4 -> x0, local copies, waits for them, and re-layouts: 2.18 us -> none
    pallas_call x1, Pallas kernels: 3.64 us -> 5.75 us  [on_plane(): pl.pallas_call(norm_kernel, grid=(CH,), out_shape=(jax.ShapeDtypeStruct((...]
where the time goes in v3:
time: 134 us
  Pallas kernels  132 us (99%)
  local copies, waits for them, and re-layouts  1.35 us (1%)
    pallas_call x1, Pallas kernels, on_plane(): pl.pallas_call(plane_kernel, out_shape=jax.ShapeDtypeStruct((8, PARTS, 64...  126 us
    pallas_call x1, Pallas kernels, on_plane(): pl.pallas_call(norm_kernel, grid=(CH,), out_shape=(jax.ShapeDtypeStruct((...  5.75 us

profile of v3, /device:TPU:1, one launch (start us, length us, event | category | flops | bytes accessed | tf_op | source)
XLA Modules:
  0.0 133.9 jit_solution(4552716351130364322)
XLA Ops:
  0.6 1.3 %copy.14.pair_ref = s32[8,2]{1,0:T(8,128)} copy(s32[8,2]{0,1:T(2,128)} %bitcast.9) | data formatting | bytes 128 | tf_op jit(solution)/shard_map/squeeze | solution.py:642
  2.0 126.2 %shard_map.131.stream_ref = bf16[8,8,64,512]{3,2,1,0:T(8,128)(2,1)} custom-call(s32[8,2]{1,0:T(8,128)} %copy.14.pair_ref, s32[1,8]{1,0:T(1,128)} %lens_ref.1, f32[2,1,2048]{2,1,0:T(1,128)} %bitcast.7, f32[64,128]{1,0:T(8,128)} %constant.6.clone.cos_ref, f32[64,128]{1,0:T(8,128)} %constant.7.clone.sin_ref, f32[1,128]{1,0:T(1,128)} %constant.8.clone.freq_ref, ...), custom_call_target="tpu_custom_call" | custom-call | tf_op jit(solution)/shard_map/pallas_call | solution.py:605
  128.1 5.7 %shard_map.132 = (bf16[4,128,1024]{2,1,0:T(8,128)(2,1)}, bf16[4,128,4096]{2,1,0:T(8,128)(2,1)}) custom-call(bf16[8,8,64,512]{3,2,1,0:T(8,128)(2,1)} %shard_map.131.stream_ref, f32[1,4096]{1,0:T(1,128)} %bitcast.8), custom_call_target="tpu_custom_call" | custom-call | tf_op jit(solution)/shard_map/pallas_call | solution.py:646

commit v4 on v3

--- a/solution.py
+++ b/solution.py
@@ -180,7 +180,7 @@
 
 
 MESH = pl.DeviceIdType.MESH
-CH = 4
+CH = 8
 PARTS = 8
 X1, Y1, Y2, S1A, S1B, S1C, XQ, XS, XM, SB, YB, XR, YR1, YR2, SR0, SR1, SR2, SR3, LN = range(19)
 KINDS = 19
@@ -248,10 +248,10 @@
     cols = pl.ds(pl.multiple_of(c * 1024, 1024), 1024)
 
     def place(g, j, at=0, count=2):
-        return grid_x.at[pl.ds(g * 8 + 2 * j + at, count), :, cols]
+        return grid_x.at[pl.ds(g * 8 + j, 1), at * 32:(at + count) * 32, cols]
 
     def own(j, at=0, count=2):
-        return cand_ref.at[2 * j + at:2 * j + at + count]
+        return cand_ref.at[j:j + 1, at * 32:(at + count) * 32]
 
     def hop(j):
         return relay.at[j:j + 1]
@@ -311,14 +311,14 @@
 
         remote(S1A, j, place(f, j), place(f, j), s_dev).wait_recv()
 
-    send_y(0)
-
-    @pl.when(jnp.logical_not(even))
-    def _():
-        for j in range(CH):
+    def send_x(j):
+        @pl.when(jnp.logical_not(even))
+        def _():
             remote(X1, j, own(j, 0, 1), place(f, j, 0, 1), x_dev).start()
 
-    send_y(1)
+    for j in range(2):
+        send_y(j)
+        send_x(j)
 
     @pl.when(even)
     def _():
@@ -333,13 +333,13 @@
         remote(XS, j, ss_own.at[j], ss_recv.at[j], x_dev).wait_recv()
         total = (ss_own[j] + ss_recv[j])[0:1, :]
         scale = lax.rsqrt(total * (1.0 / 4096.0) + epsilon)
-        column = jnp.broadcast_to(scale, (128, 256)).T
+        column = jnp.broadcast_to(scale, (128, 128)).T
         for m in range(6):
             part = slice(m * 128, (m + 1) * 128)
-            summed = q_own[4 * j:4 * j + 4, :, part].reshape(256, 128) + q_recv[
+            summed = q_own[2 * j:2 * j + 2, :, part].reshape(128, 128) + q_recv[
                 j, :, part
             ].astype(jnp.float32)
-            q_own[4 * j:4 * j + 4, :, part] = (summed * column).reshape(4, 64, 128)
+            q_own[2 * j:2 * j + 2, :, part] = (summed * column).reshape(2, 64, 128)
 
     forward_x(0)
     for j in range(CH):
@@ -348,14 +348,16 @@
             forward_x(j + 1)
         if j + 2 < CH:
             send_y(j + 2)
+            send_x(j + 2)
         finish_input(j)
 
         gain = gain1_ref[f]
+        squares = []
         for g in range(2):
-            values = grid_x[g * 8 + 2 * j:g * 8 + 2 * j + 2].reshape(128, 2048).astype(jnp.float32)
-            squares = jnp.sum(values * values, axis=1, keepdims=True)
-            ss_own[j, :, g * 128:(g + 1) * 128] = jnp.broadcast_to(squares, (128, 128)).T[0:8]
-            lhs[g * 128:(g + 1) * 128, :] = (values * gain).astype(jnp.bfloat16)
+            values = grid_x[g * 8 + j].astype(jnp.float32)
+            squares.append(jnp.sum(values * values, axis=1, keepdims=True))
+            lhs[g * 64:(g + 1) * 64, :] = (values * gain).astype(jnp.bfloat16)
+        ss_own[j] = jnp.broadcast_to(jnp.concatenate(squares, axis=0), (128, 128)).T[0:8]
 
         def project(n):
             return jnp.dot(
@@ -370,7 +372,7 @@
             at = pl.ds(pl.multiple_of(n * 256, 256), 256)
             q_send[j, :, at] = result.astype(jnp.bfloat16)
 
-        q_own[4 * j:4 * j + 4, :, 512:768] = project(4).reshape(4, 64, 256)
+        q_own[2 * j:2 * j + 2, :, 512:768] = project(4).reshape(2, 64, 256)
         remote(XQ, j, q_send.at[j], q_recv.at[j], x_dev).start()
         remote(XS, j, ss_own.at[j], ss_recv.at[j], x_dev).start()
 
@@ -378,12 +380,12 @@
         def _(n):
             result = project(n)
             at = pl.ds(pl.multiple_of(n * 256, 256), 256)
-            q_own[4 * j:4 * j + 4, :, at] = result.reshape(4, 64, 256)
-
-        if j > 1:
-            finish(j - 2)
-    finish(CH - 2)
-    finish(CH - 1)
+            q_own[2 * j:2 * j + 2, :, at] = result.reshape(2, 64, 256)
+
+        if j > 2:
+            finish(j - 3)
+    for j in range(CH - 3, CH):
+        finish(j)
     lens_copy.wait()
 
     lane = lax.broadcasted_iota(jnp.int32, (1, 128), 1)
@@ -392,7 +394,7 @@
     slot_u = lax.broadcasted_iota(jnp.int32, (128, 128), 1)
 
     def packed(cand):
-        return ((cand % 8) // 2) * 4 + (cand // 8) * 2 + cand % 2
+        return (cand % 8) * 2 + cand // 8
 
     def attention(k, half):
         row = half * 4 + k
@@ -609,15 +611,15 @@
         out_specs=hbm,
         scratch_shapes=[
             pltpu.VMEM((16, 64, 2048), bf16),
-            pltpu.VMEM((CH, 64, 1024), bf16),
-            pltpu.VMEM((256, 2048), bf16),
+            pltpu.VMEM((CH, 32, 1024), bf16),
+            pltpu.VMEM((128, 2048), bf16),
             pltpu.VMEM((2048, 1280), bf16),
             pltpu.VMEM((1024, 2048), bf16),
-            pltpu.VMEM((CH, 256, 768), bf16),
-            pltpu.VMEM((CH, 256, 768), bf16),
+            pltpu.VMEM((CH, 128, 768), bf16),
+            pltpu.VMEM((CH, 128, 768), bf16),
             pltpu.VMEM((16, 64, 768), f32),
-            pltpu.VMEM((CH, 8, 256), f32),
-            pltpu.VMEM((CH, 8, 256), f32),
+            pltpu.VMEM((CH, 8, 128), f32),
+            pltpu.VMEM((CH, 8, 128), f32),
             pltpu.VMEM((8, 128), jnp.int32),
             pltpu.VMEM((16, 128), jnp.int32),
             pltpu.VMEM((PARTS, 128, 512), bf16),
@@ -645,10 +647,10 @@
     )
     resid, normed = pl.pallas_call(
         norm_kernel,
-        grid=(CH,),
+        grid=(PARTS // 2,),
         out_shape=(
-            jax.ShapeDtypeStruct((CH, 128, 1024), bf16),
-            jax.ShapeDtypeStruct((CH, 128, 4096), bf16),
+            jax.ShapeDtypeStruct((PARTS // 2, 128, 1024), bf16),
+            jax.ShapeDtypeStruct((PARTS // 2, 128, 4096), bf16),
         ),
         in_specs=[
             pl.BlockSpec((8, 2, 64, 512), lambda k: (0, k, 0, 0)),

time: 134 us -> 140 us (1.045)
  Pallas kernels: 132 us -> 138 us
    pallas_call x1, Pallas kernels: 126 us -> 132 us  [on_plane(): pl.pallas_call(plane_kernel, out_shape=jax.ShapeDtypeStruct((8, PARTS, 64...]
where the time goes in v4:
time: 140 us
  Pallas kernels  138 us (99%)
    pallas_call x1, Pallas kernels, on_plane(): pl.pallas_call(plane_kernel, out_shape=jax.ShapeDtypeStruct((8, PARTS, 64...  132 us
    pallas_call x1, Pallas kernels, on_plane(): pl.pallas_call(norm_kernel, grid=(PARTS // 2,), out_shape=(jax.ShapeDtype...  5.75 us

profile of v4, /device:TPU:1, one launch (start us, length us, event | category | flops | bytes accessed | tf_op | source)
XLA Modules:
  0.0 140.2 jit_solution(9493939736666631527)
XLA Ops:
  0.6 1.3 copy.14.pair_ref
  2.0 132.5 %shard_map.131.stream_ref = bf16[8,8,64,512]{3,2,1,0:T(8,128)(2,1)} custom-call(s32[8,2]{1,0:T(8,128)} %copy.14.pair_ref, s32[1,8]{1,0:T(1,128)} %lens_ref.1, f32[2,1,2048]{2,1,0:T(1,128)} %bitcast.7, f32[64,128]{1,0:T(8,128)} %constant.6.clone.cos_ref, f32[64,128]{1,0:T(8,128)} %constant.7.clone.sin_ref, f32[1,128]{1,0:T(1,128)} %constant.8.clone.freq_ref, ...), custom_call_target="tpu_custom_call" | custom-call | tf_op jit(solution)/shard_map/pallas_call | solution.py:607
  134.5 5.7 %shard_map.132 = (bf16[4,128,1024]{2,1,0:T(8,128)(2,1)}, bf16[4,128,4096]{2,1,0:T(8,128)(2,1)}) custom-call(bf16[8,8,64,512]{3,2,1,0:T(8,128)(2,1)} %shard_map.131.stream_ref, f32[1,4096]{1,0:T(1,128)} %bitcast.8), custom_call_target="tpu_custom_call" | custom-call | tf_op jit(solution)/shard_map/pallas_call | solution.py:648

commit v5 on v3

--- a/solution.py
+++ b/solution.py
@@ -319,6 +319,7 @@
             remote(X1, j, own(j, 0, 1), place(f, j, 0, 1), x_dev).start()
 
     send_y(1)
+    send_y(2)
 
     @pl.when(even)
     def _():
@@ -342,12 +343,9 @@
             q_own[4 * j:4 * j + 4, :, part] = (summed * column).reshape(4, 64, 128)
 
     forward_x(0)
+    forward_y(0)
+    forward_x(1)
     for j in range(CH):
-        forward_y(j)
-        if j + 1 < CH:
-            forward_x(j + 1)
-        if j + 2 < CH:
-            send_y(j + 2)
         finish_input(j)
 
         gain = gain1_ref[f]
@@ -373,6 +371,13 @@
         q_own[4 * j:4 * j + 4, :, 512:768] = project(4).reshape(4, 64, 256)
         remote(XQ, j, q_send.at[j], q_recv.at[j], x_dev).start()
         remote(XS, j, ss_own.at[j], ss_recv.at[j], x_dev).start()
+
+        if j + 1 < CH:
+            forward_y(j + 1)
+        if j + 2 < CH:
+            forward_x(j + 2)
+        if j + 3 < CH:
+            send_y(j + 3)
 
         @pl.loop(0, 2)
         def _(n):

time: 134 us -> 138 us (1.030)
  Pallas kernels: 132 us -> 136 us
    pallas_call x1, Pallas kernels: 126 us -> 130 us  [on_plane(): pl.pallas_call(plane_kernel, out_shape=jax.ShapeDtypeStruct((8, PARTS, 64...]
where the time goes in v5:
time: 138 us
  Pallas kernels  136 us (99%)
    pallas_call x1, Pallas kernels, on_plane(): pl.pallas_call(plane_kernel, out_shape=jax.ShapeDtypeStruct((8, PARTS, 64...  130 us
    pallas_call x1, Pallas kernels, on_plane(): pl.pallas_call(norm_kernel, grid=(CH,), out_shape=(jax.ShapeDtypeStruct((...  5.75 us

profile of v5, /device:TPU:1, one launch (start us, length us, event | category | flops | bytes accessed | tf_op | source)
XLA Modules:
  0.0 137.9 jit_solution(10910773672588952506)
XLA Ops:
  0.6 1.3 copy.14.pair_ref
  2.0 130.2 %shard_map.131.stream_ref = bf16[8,8,64,512]{3,2,1,0:T(8,128)(2,1)} custom-call(s32[8,2]{1,0:T(8,128)} %copy.14.pair_ref, s32[1,8]{1,0:T(1,128)} %lens_ref.1, f32[2,1,2048]{2,1,0:T(1,128)} %bitcast.7, f32[64,128]{1,0:T(8,128)} %constant.6.clone.cos_ref, f32[64,128]{1,0:T(8,128)} %constant.7.clone.sin_ref, f32[1,128]{1,0:T(1,128)} %constant.8.clone.freq_ref, ...), custom_call_target="tpu_custom_call" | custom-call | tf_op jit(solution)/shard_map/pallas_call | solution.py:610
  132.1 5.7 %shard_map.132 = (bf16[4,128,1024]{2,1,0:T(8,128)(2,1)}, bf16[4,128,4096]{2,1,0:T(8,128)(2,1)}) custom-call(bf16[8,8,64,512]{3,2,1,0:T(8,128)(2,1)} %shard_map.131.stream_ref, f32[1,4096]{1,0:T(1,128)} %bitcast.8), custom_call_target="tpu_custom_call" | custom-call | tf_op jit(solution)/shard_map/pallas_call | solution.py:651

commit v6 on v3

--- a/solution.py
+++ b/solution.py
@@ -318,8 +318,6 @@
         for j in range(CH):
             remote(X1, j, own(j, 0, 1), place(f, j, 0, 1), x_dev).start()
 
-    send_y(1)
-
     @pl.when(even)
     def _():
         for j in range(CH):
@@ -342,6 +340,7 @@
             q_own[4 * j:4 * j + 4, :, part] = (summed * column).reshape(4, 64, 128)
 
     forward_x(0)
+    send_y(1)
     for j in range(CH):
         forward_y(j)
         if j + 1 < CH:

time: 134 us -> 134 us (level)
  no operation moved by 1% of the time
where the time goes in v6:
time: 134 us
  Pallas kernels  132 us (99%)
  local copies, waits for them, and re-layouts  1.35 us (1%)
    pallas_call x1, Pallas kernels, on_plane(): pl.pallas_call(plane_kernel, out_shape=jax.ShapeDtypeStruct((8, PARTS, 64...  126 us
    pallas_call x1, Pallas kernels, on_plane(): pl.pallas_call(norm_kernel, grid=(CH,), out_shape=(jax.ShapeDtypeStruct((...  5.75 us

profile of v6, /device:TPU:1, one launch (start us, length us, event | category | flops | bytes accessed | tf_op | source)
XLA Modules:
  0.0 133.8 jit_solution(711856897631390279)
XLA Ops:
  0.6 1.3 %copy.14.pair_ref = s32[8,2]{1,0:T(8,128)} copy(s32[8,2]{0,1:T(2,128)} %bitcast.9) | data formatting | bytes 128 | tf_op jit(solution)/shard_map/squeeze | solution.py:641
  2.0 126.1 %shard_map.131.stream_ref = bf16[8,8,64,512]{3,2,1,0:T(8,128)(2,1)} custom-call(s32[8,2]{1,0:T(8,128)} %copy.14.pair_ref, s32[1,8]{1,0:T(1,128)} %lens_ref.1, f32[2,1,2048]{2,1,0:T(1,128)} %bitcast.7, f32[64,128]{1,0:T(8,128)} %constant.6.clone.cos_ref, f32[64,128]{1,0:T(8,128)} %constant.7.clone.sin_ref, f32[1,128]{1,0:T(1,128)} %constant.8.clone.freq_ref, ...), custom_call_target="tpu_custom_call" | custom-call | tf_op jit(solution)/shard_map/pallas_call | solution.py:604
  128.1 5.7 %shard_map.132 = (bf16[4,128,1024]{2,1,0:T(8,128)(2,1)}, bf16[4,128,4096]{2,1,0:T(8,128)(2,1)}) custom-call(bf16[8,8,64,512]{3,2,1,0:T(8,128)(2,1)} %shard_map.131.stream_ref, f32[1,4096]{1,0:T(1,128)} %bitcast.8), custom_call_target="tpu_custom_call" | custom-call | tf_op jit(solution)/shard_map/pallas_call | solution.py:645
